TPU v7x, 768 devices: a whole 4x8x12 slice. The times are simulated.
768 devices in a mesh: dp: 192 (over y, z_lo, x, core), fsdp: 4 (over z_hi).
Axes of the slice: x: 4, y: 8, z: 12 (z_hi: 4, z_lo: 3; z = z_hi * 3 + z_lo), core: 2. Of those that a mesh axis runs over, the one named last changes fastest.
Arguments:
- queries: bfloat16 [98304, 2048], P(('dp', 'fsdp')), may hold values from -100 to 100
- keys: bfloat16 [98304, 2048], P(('dp', 'fsdp')), may hold values from -4 to 4
- values: bfloat16 [98304, 2048], P(('dp', 'fsdp')), may hold values from -6 to 6
- doc_mask: int32 [98304, 384], P(('dp', 'fsdp')), may hold values from 0 to 1, as said below
- ratio_bins: int32 [98304], P(('dp', 'fsdp')), may hold values from 0 to 7
- out_grad: bfloat16 [98304, 2048], P(('dp', 'fsdp')), may hold values from -6 to 6
Outputs:
- attended: bfloat16 [98304, 2048], P(('dp', 'fsdp'))
- query_grad: bfloat16 [98304, 2048], P(('dp', 'fsdp'))
- key_grad: bfloat16 [98304, 2048], P(('dp', 'fsdp'))
- value_grad: bfloat16 [98304, 2048], P(('dp', 'fsdp'))
Inputs may be any that keep to these rules, and one draw needn't show every extreme that they name: `doc_mask`: entry (i, c) is 1 exactly where key position g = (i // 128) * 128 - 128 + c exists and lies in the same packed document as token i; every token marks itself, and no document spans more than two neighbouring devices.
All inputs are finite; a program needn't handle non-finite values.
Results may differ from a plain program's by a relative error of at most 0.04.
Values may be sent and summed in bfloat16 or wider, within the bound.
A program may use at most 64 MiB of HBM per device.

v0:
```python
import math

import jax
import jax.numpy as jnp
from jax import lax
from jax.sharding import PartitionSpec as P

HEADS = 16
HEAD_DIM = 128
NBINS = 8


masked_score = -1e30


def with_halo(cells, sides, width):
    for axis, dim in sides:
        count = lax.axis_size(axis)
        ends = count - 1
        head = lax.slice_in_dim(cells, 0, width, axis=dim)
        tail = lax.slice_in_dim(cells, cells.shape[dim] - width, cells.shape[dim], axis=dim)
        cells = jnp.concatenate(
            [
                lax.ppermute(tail, axis, [(i, (i + 1) % count) for i in range(ends)]),
                cells,
                lax.ppermute(head, axis, [((i + 1) % count, i) for i in range(ends)]),
            ],
            axis=dim,
        )
    return cells


def passed_along(shard, axis, by):
    peers = lax.axis_size(axis)
    pairs = [(i, i + by) for i in range(peers) if 0 <= i + by < peers]
    return lax.ppermute(shard, axis, pairs)


def split_heads(matrix):
    return matrix.reshape(matrix.shape[0], HEADS, -1)


def head_scores(query_rows, key_rows, allowed):
    score_scale = 1.0 / math.sqrt(HEAD_DIM)
    scores = (
        jnp.einsum(
            "ihd,jhd->hij",
            split_heads(query_rows),
            split_heads(key_rows),
            preferred_element_type=jnp.float32,
        )
        * score_scale
    )
    return jnp.where(allowed[None], scores, masked_score)


def local(queries, keys, values, doc_mask, ratio_bins, out_grad):
    rows_here = queries.shape[0]
    width = queries.shape[1]
    score_scale = 1.0 / math.sqrt(HEAD_DIM)
    allowed = doc_mask == 1
    weight = NBINS / (ratio_bins.astype(jnp.float32) + 1.0)
    scaled = (out_grad.astype(jnp.float32) * weight[:, None]).astype(jnp.bfloat16)
    window = with_halo(jnp.stack([keys, values]), ((("dp", "fsdp"), 1),), rows_here)
    key_window = window[0]
    value_window = window[1]
    scores = head_scores(queries, key_window, allowed)
    largest = jnp.max(scores, axis=2, keepdims=True)
    log_total = largest + jnp.log(jnp.sum(jnp.exp(scores - largest), axis=2, keepdims=True))
    softmax_w = jnp.exp(scores - log_total)
    rounded_w = softmax_w.astype(jnp.bfloat16)
    attended = jnp.einsum(
        "hij,jhd->ihd", rounded_w, split_heads(value_window), preferred_element_type=jnp.float32
    )
    attended = attended.reshape(rows_here, width).astype(jnp.bfloat16)
    delta = jnp.transpose(
        jnp.sum(
            split_heads(scaled).astype(jnp.float32) * split_heads(attended).astype(jnp.float32),
            axis=2,
        )
    )
    dprob = jnp.einsum(
        "ihd,jhd->hij",
        split_heads(scaled),
        split_heads(value_window),
        preferred_element_type=jnp.float32,
    )
    dscore = (softmax_w * (dprob - delta[:, :, None])).astype(jnp.bfloat16)
    query_grad = (
        jnp.einsum(
            "hij,jhd->ihd", dscore, split_heads(key_window), preferred_element_type=jnp.float32
        )
        * score_scale
    )
    query_grad = query_grad.reshape(rows_here, width).astype(jnp.bfloat16)
    key_terms = (
        jnp.einsum("hij,ihd->jhd", dscore, split_heads(queries), preferred_element_type=jnp.float32)
        * score_scale
    )
    value_terms = jnp.einsum(
        "hij,ihd->jhd", rounded_w, split_heads(scaled), preferred_element_type=jnp.float32
    )
    grad_terms = jnp.stack(
        [key_terms.reshape(3 * rows_here, width), value_terms.reshape(3 * rows_here, width)]
    )
    summed = grad_terms[:, rows_here : 2 * rows_here]
    for shift_by, outgoing in (
        (1, grad_terms[:, 2 * rows_here :]),
        (-1, grad_terms[:, :rows_here]),
    ):
        summed = summed + passed_along(outgoing, ("dp", "fsdp"), shift_by)
    key_grad = summed[0].astype(jnp.bfloat16)
    value_grad = summed[1].astype(jnp.bfloat16)
    return (attended, query_grad, key_grad, value_grad)


def solution(mesh):
    placed = (
        P(("dp", "fsdp"), None),
        P(("dp", "fsdp"), None),
        P(("dp", "fsdp"), None),
        P(("dp", "fsdp"), None),
        P(("dp", "fsdp")),
        P(("dp", "fsdp"), None),
    )
    return jax.shard_map(
        local,
        mesh=mesh,
        in_specs=placed,
        out_specs=(
            P(("dp", "fsdp"), None),
            P(("dp", "fsdp"), None),
            P(("dp", "fsdp"), None),
            P(("dp", "fsdp"), None),
        ),
        check_vma=False,
    )
```

profile of v0, /device:TPU:56, one launch (start us, length us, event | category | flops | bytes accessed | tf_op | source)
XLA Modules:
  0.0 260.3 jit_solution(4621169380648300464)
XLA Ops:
  0.7 1.4 copy.27
  2.0 1.3 copy.28
  3.5 17.0 %collective-permute-start.1 = (bf16[2,128,2048]{1,2,0:T(8,128)(2,1)S(1)}, bf16[2,128,2048]{1,2,0:T(8,128)(2,1)}, u32[]{:S(2)}, u32[]{:S(2)}) collective-permute-start(bf16[2,128,2048]{1,2,0:T(8,128)(2,1)S(1)} %pad_maximum_fusion.2), channel_id=1, source_target_pairs={{1,0},{2,1},{3,2},{4,3},{5,4},{6,5},{7,6},{8,7},{9,8},{10,9},{11,1... | collective-permute-start | bytes 3145736 | tf_op jit(solution)/shard_map/ppermute | solution.py:26
  20.5 1.9 collective-permute-start
  23.1 1.5 copy.56
  24.6 61.3 %collective-permute-done.1 = bf16[2,128,2048]{1,2,0:T(8,128)(2,1)} collective-permute-done((bf16[2,128,2048]{1,2,0:T(8,128)(2,1)S(1)}, bf16[2,128,2048]{1,2,0:T(8,128)(2,1)}, u32[]{:S(2)}, u32[]{:S(2)}) %collective-permute-start.1) | collective-permute-done | bytes 1048608 | tf_op jit(solution)/shard_map/ppermute | solution.py:26
  85.9 10.8 %collective-permute-done = bf16[2,128,2048]{1,2,0:T(8,128)(2,1)} collective-permute-done((bf16[2,128,2048]{1,2,0:T(8,128)(2,1)S(1)}, bf16[2,128,2048]{1,2,0:T(8,128)(2,1)}, u32[]{:S(2)}, u32[]{:S(2)}) %collective-permute-start) | collective-permute-done | bytes 1048608 | tf_op jit(solution)/shard_map/ppermute | solution.py:24
  96.7 1.7 pad_maximum_fusion
  100.4 1.9 multiply_reduce_fusion
  102.3 2.0 fusion.8
  104.4 1.4 multiply_convert_fusion
  105.7 1.1 copy-done.2
  106.9 2.2 multiply_bitcast_fusion
  109.1 3.5 %copy.41 = f32[384,16,128]{0,2,1:T(8,128)} copy(f32[384,16,128]{2,0,1:T(8,128)} %multiply_bitcast_fusion) | data formatting | bytes 6291456 | tf_op jit(solution)/shard_map/mul | solution.py:97
  112.7 4.0 %fusion.1 = (f32[2,128,2048]{1,2,0:T(8,128)}, f32[2,128,2048]{1,2,0:T(8,128)}) fusion(f32[1,384,2048]{1,2,0:T(8,128)} %bitcast.51, f32[1,384,2048]{1,2,0:T(8,128)S(1)} %bitcast.49), kind=kLoop, calls=%fused_computation.11 | loop fusion | flops 1048576 | bytes 10485760 | tf_op jit(solution)/shard_map/stack | solution.py:103
  116.7 1.9 collective-permute-start.2
  118.6 7.9 %collective-permute-start.3 = (f32[2,128,2048]{1,2,0:T(8,128)}, f32[2,128,2048]{1,2,0:T(8,128)}, u32[]{:S(2)}, u32[]{:S(2)}) collective-permute-start(f32[2,128,2048]{1,2,0:T(8,128)} %get-tuple-element.13), channel_id=1, source_target_pairs={{1,0},{2,1},{3,2},{4,3},{5,4},{6,5},{7,6},{8,7},{9,8},{10,9},{11,1... | collective-permute-start | bytes 6291464 | tf_op jit(solution)/shard_map/ppermute | solution.py:36
  126.5 1.4 fusion.7
  127.9 2.0 copy.44
  129.9 2.0 copy.43
  132.0 122.7 %collective-permute-done.2 = f32[2,128,2048]{1,2,0:T(8,128)} collective-permute-done((f32[2,128,2048]{1,2,0:T(8,128)}, f32[2,128,2048]{1,2,0:T(8,128)}, u32[]{:S(2)}, u32[]{:S(2)}) %collective-permute-start.2) | collective-permute-done | bytes 2097184 | tf_op jit(solution)/shard_map/ppermute | solution.py:36
  255.5 2.8 %fusion.5 = bf16[2,128,2048]{1,2,0:T(8,128)(2,1)S(1)} fusion(f32[2,128,2048]{1,2,0:T(8,128)} %collective-permute-done.3, f32[2,128,2048]{1,2,0:T(8,128)} %collective-permute-done.2, f32[1,384,2048]{1,2,0:T(8,128)} %bitcast.52, f32[1,384,2048]{1,2,0:T(8,128)S(1)} %bitcast.50), kind=kLoop, calls=%fused_computation.15 | loop fusion | flops 2097152 | bytes 11534336 | tf_op jit(solution)/shard_map/convert.2
  258.3 1.0 copy.46
  259.3 1.0 copy.45
  (33 shorter events, 3.4 us)
Async XLA Ops:
  0.6 21.8 %copy-start.9 = (s32[128,384]{1,0:T(8,128)S(1)}, s32[128,384]{1,0:T(8,128)}, u32[]{:S(2)}) copy-start(s32[128,384]{1,0:T(8,128)} %param.9) | copy-start | bytes 589828
  0.6 22.0 %copy-start.10 = (s32[128]{0:T(128)S(1)}, s32[128]{0:T(128)}, u32[]{:S(2)}) copy-start(s32[128]{0:T(128)} %param.10) | copy-start | bytes 1540
  0.7 22.0 %copy-start.8 = (bf16[128,2048]{1,0:T(8,128)(2,1)S(1)}, bf16[128,2048]{1,0:T(8,128)(2,1)}, u32[]{:S(2)}) copy-start(bf16[128,2048]{1,0:T(8,128)(2,1)} %param.11) | copy-start | bytes 1572868
  3.5 82.5 %collective-permute-start.1 = (bf16[2,128,2048]{1,2,0:T(8,128)(2,1)S(1)}, bf16[2,128,2048]{1,2,0:T(8,128)(2,1)}, u32[]{:S(2)}, u32[]{:S(2)}) collective-permute-start(bf16[2,128,2048]{1,2,0:T(8,128)(2,1)S(1)} %pad_maximum_fusion.2), channel_id=1, source_target_pairs={{1,0},{2,1},{3,2},{4,3},{5,4},{6,5},{7,6},{8,7},{9,8},{10,9},{11,1... | collective-permute-start | bytes 3145736 | tf_op jit(solution)/shard_map/ppermute | solution.py:26
  20.5 76.2 %collective-permute-start = (bf16[2,128,2048]{1,2,0:T(8,128)(2,1)S(1)}, bf16[2,128,2048]{1,2,0:T(8,128)(2,1)}, u32[]{:S(2)}, u32[]{:S(2)}) collective-permute-start(bf16[2,128,2048]{1,2,0:T(8,128)(2,1)S(1)} %pad_maximum_fusion.2), channel_id=1, source_target_pairs={{0,1},{1,2},{2,3},{3,4},{4,5},{5,6},{6,7},{7,8},{8,9},{9,10},{10,1... | collective-permute-start | bytes 3145736 | tf_op jit(solution)/shard_map/ppermute | solution.py:24
  23.1 77.3 %copy-start.6 = (bf16[128,2048]{0,1:T(8,128)(2,1)}, bf16[128,2048]{0,1:T(8,128)(2,1)S(1)}, u32[]{:S(2)}) copy-start(bf16[128,2048]{0,1:T(8,128)(2,1)S(1)} %copy.33) | copy-start | bytes 1572868
  24.6 74.2 %copy-start.4 = (bf16[128,2048]{0,1:T(8,128)(2,1)}, bf16[128,2048]{0,1:T(8,128)(2,1)S(1)}, u32[]{:S(2)}) copy-start(bf16[128,2048]{0,1:T(8,128)(2,1)S(1)} %copy.56) | copy-start | bytes 1572868
  98.8 1.5 copy-start
  102.3 2.1 copy-start.7
  104.3 2.5 copy-start.5
  105.7 1.2 copy-start.2
  112.6 13.8 %copy-start.1 = (bf16[1,384,2048]{1,2,0:T(8,128)(2,1)S(1)}, bf16[1,384,2048]{1,2,0:T(8,128)(2,1)}, u32[]{:S(2)}) copy-start(bf16[1,384,2048]{1,2,0:T(8,128)(2,1)} %copy-done) | copy-start | bytes 4718596
  112.6 13.8 %copy-start.3 = (bf16[16,128,384]{1,2,0:T(8,128)(2,1)S(1)}, bf16[16,128,384]{1,2,0:T(8,128)(2,1)}, u32[]{:S(2)}) copy-start(bf16[16,128,384]{1,2,0:T(8,128)(2,1)} %copy-done.2) | copy-start | bytes 4718596
  116.7 138.0 %collective-permute-start.2 = (f32[2,128,2048]{1,2,0:T(8,128)}, f32[2,128,2048]{1,2,0:T(8,128)}, u32[]{:S(2)}, u32[]{:S(2)}) collective-permute-start(f32[2,128,2048]{1,2,0:T(8,128)} %get-tuple-element.12), channel_id=1, source_target_pairs={{0,1},{1,2},{2,3},{3,4},{4,5},{5,6},{6,7},{7,8},{8,9},{9,10},{10,1... | collective-permute-start | bytes 6291464 | tf_op jit(solution)/shard_map/ppermute | solution.py:36
  118.6 136.8 %collective-permute-start.3 = (f32[2,128,2048]{1,2,0:T(8,128)}, f32[2,128,2048]{1,2,0:T(8,128)}, u32[]{:S(2)}, u32[]{:S(2)}) collective-permute-start(f32[2,128,2048]{1,2,0:T(8,128)} %get-tuple-element.13), channel_id=1, source_target_pairs={{1,0},{2,1},{3,2},{4,3},{5,4},{6,5},{7,6},{8,7},{9,8},{10,9},{11,1... | collective-permute-start | bytes 6291464 | tf_op jit(solution)/shard_map/ppermute | solution.py:36
where the time goes:
time: 261 us; the launch traced here: 260 us
  waiting for transfers between devices  196 us (75%)
  starting transfers between devices  28.7 us (11%)
  local copies, waits for them, and re-layouts  15.8 us (6%)
  matrix products  9.78 us (4%)
  other arithmetic  9.51 us (4%)
    ppermute x2, waiting for transfers between devices, passed_along(): return lax.ppermute(shard, axis, pairs)  123 us
    ppermute x1, waiting for transfers between devices, with_halo(): lax.ppermute(head, axis, [((i + 1) % count, i) for i in range(ends)])  61.3 us
    ppermute x1, starting transfers between devices, with_halo(): lax.ppermute(head, axis, [((i + 1) % count, i) for i in range(ends)])  17 us
    ppermute x1, waiting for transfers between devices, with_halo(): lax.ppermute(tail, axis, [(i, (i + 1) % count) for i in range(ends)])  10.8 us
    unnamed x28, local copies, waits for them, and re-layouts  9.99 us
    ppermute x2, starting transfers between devices, passed_along(): return lax.ppermute(shard, axis, pairs)  9.77 us
  transfers between devices with their start and end apart: 4, of which 4 were waited for; matrix products, arithmetic and copies ran while one was open for 3% of the time, Pallas kernels for 0%

commit v1 on v0

v1 whole, which is shorter than its diff:
```python
import functools
import math

import jax
import jax.numpy as jnp
from jax import lax
from jax.experimental import pallas as pl
from jax.experimental.pallas import tpu as pltpu
from jax.sharding import PartitionSpec as P

HEADS = 16
HEAD_DIM = 128
NBINS = 8
GROUP = 2
GROUPS = HEADS // GROUP
COLS = GROUP * HEAD_DIM
MASKED = -1e30
MESH = pl.DeviceIdType.MESH


def neighbour(step):
    dps, fsdps = lax.axis_size("dp"), lax.axis_size("fsdp")
    flat = lax.axis_index("dp") * fsdps + lax.axis_index("fsdp")
    flat = lax.rem(flat + step + dps * fsdps, dps * fsdps)
    return (flat // fsdps, lax.rem(flat, fsdps))


def dot(a, b, dims):
    return lax.dot_general(a, b, (dims, ((), ())), preferred_element_type=jnp.float32)


def kernel(
    queries, keys, values, out_grad, mask, bins,
    attended, query_grad, key_grad, value_grad,
    q_v, k_v, v_v, g_v, halo, sent, got, own, bias, weight,
    load_sem, halo_send, halo_recv, term_send, term_recv,
):
    scale = 1.0 / math.sqrt(HEAD_DIM)
    rows = q_v.shape[0]
    sides = (neighbour(-1), neighbour(1))

    def load(at, src, dst):
        return pltpu.make_async_copy(src, dst, load_sem.at[at])

    loads = [
        load(0, queries, q_v), load(1, keys, k_v), load(2, values, v_v), load(3, out_grad, g_v)
    ]
    for copy in loads:
        copy.start()

    barrier = pltpu.get_barrier_semaphore()
    for side in sides:
        pl.semaphore_signal(barrier, inc=1, device_id=side, device_id_type=MESH)
    pl.semaphore_wait(barrier, 2)

    def columns(group):
        return pl.ds(pl.multiple_of(group * COLS, COLS), COLS)

    def halo_copy(group, kind, side):
        src = (keys, values)[kind]
        at = (kind * 2 + 1 - side) * GROUPS + group
        return pltpu.make_async_remote_copy(
            src_ref=src.at[:, columns(group)],
            dst_ref=halo.at[kind, 1 - side, :, columns(group)],
            send_sem=halo_send.at[at],
            recv_sem=halo_recv.at[at],
            device_id=sides[side],
            device_id_type=MESH,
        )

    def term_copy(group, kind, side):
        at = (kind * 2 + 1 - side) * GROUPS + group
        return pltpu.make_async_remote_copy(
            src_ref=sent.at[kind, side, :, columns(group)],
            dst_ref=got.at[kind, 1 - side, :, columns(group)],
            send_sem=term_send.at[at],
            recv_sem=term_recv.at[at],
            device_id=sides[side],
            device_id_type=MESH,
        )

    each = [(kind, side) for kind in range(2) for side in range(2)]

    def send_halo(group, carry):
        for kind, side in each:
            halo_copy(group, kind, side).start()
        return carry

    lax.fori_loop(0, GROUPS, send_halo, 0)

    bias[...] = jnp.where(mask[...] == 1, 0.0, MASKED)
    ratio = NBINS / (bins[...].astype(jnp.float32) + 1.0)
    weight[...] = jnp.broadcast_to(ratio, (HEAD_DIM, rows)).T
    for copy in loads:
        copy.wait()

    def attend(group, carry):
        for kind, side in each:
            halo_copy(group, kind, side).wait_recv()
        for head in range(GROUP):
            here = pl.ds(
                pl.multiple_of(group * COLS + head * HEAD_DIM, HEAD_DIM), HEAD_DIM
            )
            q = q_v[:, here]
            g = (g_v[:, here].astype(jnp.float32) * weight[...]).astype(jnp.bfloat16)
            k = jnp.concatenate([halo[0, 0, :, here], k_v[:, here], halo[0, 1, :, here]], axis=0)
            v = jnp.concatenate([halo[1, 0, :, here], v_v[:, here], halo[1, 1, :, here]], axis=0)
            allowed = bias[...] == 0.0
            scores = jnp.where(allowed, dot(q, k, ((1,), (1,))) * scale, MASKED)
            largest = jnp.max(scores, axis=1, keepdims=True)
            powers = jnp.exp(scores - largest)
            prob = powers / jnp.sum(powers, axis=1, keepdims=True)
            prob_w = prob.astype(jnp.bfloat16)
            out = dot(prob_w, v, ((1,), (0,))).astype(jnp.bfloat16)
            attended[:, here] = out
            delta = jnp.sum(
                g.astype(jnp.float32) * out.astype(jnp.float32), axis=1, keepdims=True
            )
            dprob = dot(g, v, ((1,), (1,)))
            dscore = (prob * (dprob - delta)).astype(jnp.bfloat16)
            query_grad[:, here] = (dot(dscore, k, ((1,), (0,))) * scale).astype(jnp.bfloat16)
            dk = dot(dscore, q, ((0,), (0,))) * scale
            dv = dot(prob_w, g, ((0,), (0,)))
            for kind, term in ((0, dk), (1, dv)):
                sent[kind, 0, :, here] = term[:rows].astype(jnp.bfloat16)
                own[kind, :, here] = term[rows : 2 * rows]
                sent[kind, 1, :, here] = term[2 * rows :].astype(jnp.bfloat16)
        for kind, side in each:
            term_copy(group, kind, side).start()
        return carry

    lax.fori_loop(0, GROUPS, attend, 0)

    def finish(group, carry):
        for kind, side in each:
            term_copy(group, kind, side).wait_recv()
        for kind, grad in ((0, key_grad), (1, value_grad)):
            here = columns(group)
            total = own[kind, :, here] + got[kind, 0, :, here].astype(jnp.float32)
            grad[:, here] = (total + got[kind, 1, :, here].astype(jnp.float32)).astype(jnp.bfloat16)
        return carry

    lax.fori_loop(0, GROUPS, finish, 0)

    def drain(group, carry):
        for kind, side in each:
            halo_copy(group, kind, side).wait_send()
            term_copy(group, kind, side).wait_send()
        return carry

    lax.fori_loop(0, GROUPS, drain, 0)


def local(queries, keys, values, doc_mask, ratio_bins, out_grad):
    rows, width = queries.shape
    result = jax.ShapeDtypeStruct((rows, width), jnp.bfloat16)
    any_space = pl.BlockSpec(memory_space=pl.ANY)
    vmem = pl.BlockSpec(memory_space=pltpu.VMEM)
    block = pltpu.VMEM((rows, width), jnp.bfloat16)
    return pl.pallas_call(
        kernel,
        out_shape=[result] * 4,
        in_specs=[any_space] * 4 + [vmem] * 2,
        out_specs=[vmem] * 4,
        scratch_shapes=[
            block, block, block, block,
            pltpu.VMEM((2, 2, rows, width), jnp.bfloat16),
            pltpu.VMEM((2, 2, rows, width), jnp.bfloat16),
            pltpu.VMEM((2, 2, rows, width), jnp.bfloat16),
            pltpu.VMEM((2, rows, width), jnp.float32),
            pltpu.VMEM(doc_mask.shape, jnp.float32),
            pltpu.VMEM((rows, HEAD_DIM), jnp.float32),
            pltpu.SemaphoreType.DMA((4,)),
            pltpu.SemaphoreType.DMA((4 * GROUPS,)),
            pltpu.SemaphoreType.DMA((4 * GROUPS,)),
            pltpu.SemaphoreType.DMA((4 * GROUPS,)),
            pltpu.SemaphoreType.DMA((4 * GROUPS,)),
        ],
        compiler_params=pltpu.CompilerParams(
            collective_id=0, has_side_effects=True, vmem_limit_bytes=40 * 2**20
        ),
        cost_estimate=pl.CostEstimate(
            flops=12 * HEADS * rows * 3 * rows * HEAD_DIM,
            bytes_accessed=16 * rows * width,
            transcendentals=HEADS * rows * 3 * rows,
        ),
    )(queries, keys, values, out_grad, doc_mask, ratio_bins.reshape(1, rows))


def solution(mesh):
    split = P(("dp", "fsdp"), None)
    return jax.shard_map(
        local,
        mesh=mesh,
        in_specs=(split, split, split, split, P(("dp", "fsdp")), split),
        out_specs=(split, split, split, split),
        check_vma=False,
    )
```

time: 261 us -> 165 us (0.63)
  waiting for transfers between devices: 196 us -> 0 us
  Pallas kernels: 0 us -> 153 us
  starting transfers between devices: 28.7 us -> 0 us
  matrix products: 9.78 us -> 0 us
  other arithmetic: 9.51 us -> 0 us
  local copies, waits for them, and re-layouts: 15.8 us -> 8.91 us
    ppermute x4 -> x0, waiting for transfers between devices: 196 us -> none  [the longest x2 123 us: passed_along(): return lax.ppermute(shard, axis, pairs)]
    pallas_call x0 -> x1, Pallas kernels: none -> 153 us  [local(): pl.pallas_call(kernel, out_shape=[result] * 4, in_specs=[any_space] * 4 +...]
    ppermute x4 -> x0, starting transfers between devices: 28.7 us -> none  [the longest x1 17 us: with_halo(): lax.ppermute(head, axis, [((i + 1) % count, i) for i in range(ends)])]
    dot_general x6 -> x0, matrix products: 9.78 us -> none  [the longest x1 2.25 us: local(): jnp.einsum('hij,ihd->jhd', dscore, split_heads(queries), preferred_elemen...]
    another operation x3 -> x0, other arithmetic: 6.91 us -> none  [the longest x1 4.04 us: local(): jnp.stack([key_terms.reshape(3 * rows_here, width), value_terms.reshape(3...]
    mul x1 -> x0, local copies, waits for them, and re-layouts: 3.52 us -> none  [local(): jnp.einsum('hij,ihd->jhd', dscore, split_heads(queries), preferred_elemen...]
    unnamed x28 -> x16, local copies, waits for them, and re-layouts: 9.99 us -> 8.91 us
  transfers between devices with their start and end apart: 4 -> 0, of which waited for: 4 -> 0; matrix products, arithmetic and copies ran while one was open for 3% -> 0% of each run, Pallas kernels for 0% -> 0%
where the time goes in v1:
time: 165 us; the launch traced here: 163 us
  Pallas kernels  153 us (93%)
  local copies, waits for them, and re-layouts  8.91 us (5%)
    pallas_call x1, Pallas kernels, local(): pl.pallas_call(kernel, out_shape=[result] * 4, in_specs=[any_space] * 4 +...  153 us
    unnamed x16, local copies, waits for them, and re-layouts  8.91 us

profile of v1, /device:TPU:56, one launch (start us, length us, event | category | flops | bytes accessed | tf_op | source)
XLA Modules:
  0.0 162.5 jit_solution(5313567675584247595)
XLA Ops:
  0.6 0.0 copy-start.5
  0.6 0.6 copy-done.5
  1.3 0.0 copy-start
  1.3 1.0 copy-done
  2.3 0.0 copy-start.1
  2.3 1.0 copy-done.1
  3.4 0.0 copy-start.2
  3.4 1.0 copy-done.2
  4.4 0.0 copy-start.3
  4.4 1.0 copy-done.3
  5.5 0.0 copy-start.4
  5.5 0.9 copy-done.4
  6.4 153.0 %shard_map.93 = (bf16[128,2048]{1,0:T(8,128)(2,1)S(1)}, bf16[128,2048]{1,0:T(8,128)(2,1)S(1)}, bf16[128,2048]{1,0:T(8,128)(2,1)S(1)}, bf16[128,2048]{1,0:T(8,128)(2,1)S(1)}) custom-call(bf16[128,2048]{1,0:T(8,128)(2,1)S(1)} %copy-done, bf16[128,2048]{1,0:T(8,128)(2,1)S(1)} %copy-done.1, bf16[128,2048]{1,0:T(8,128)(2,1)S(1)} %copy-done.2, ...), custom_call_target="tpu_custom_call" | custom-call | flops 1207959552 | bytes 4194304 | tf_op jit(solution)/shard_map/pallas_call | solution.py:160
  159.4 0.8 copy.14
  160.2 0.8 copy.15
  160.9 0.8 copy.16
  161.7 0.8 copy.17
Async XLA Ops:
  0.6 0.7 copy-start.5
  1.3 1.0 copy-start
  2.3 1.0 copy-start.1
  3.4 1.0 copy-start.2
  4.4 1.0 copy-start.3
  5.5 0.9 copy-start.4

commit v2 on v1

--- a/solution.py
+++ b/solution.py
@@ -15,6 +15,7 @@
 GROUPS = HEADS // GROUP
 COLS = GROUP * HEAD_DIM
 MASKED = -1e30
+PIECES = 4
 MESH = pl.DeviceIdType.MESH
 
 
@@ -31,9 +32,9 @@
 
 def kernel(
     queries, keys, values, out_grad, mask, bins,
-    attended, query_grad, key_grad, value_grad,
-    q_v, k_v, v_v, g_v, halo, sent, got, own, bias, weight,
-    load_sem, halo_send, halo_recv, term_send, term_recv,
+    attended_hbm, query_grad_hbm, key_grad_hbm, value_grad_hbm,
+    attended, query_grad, key_grad, value_grad, q_v, k_v, v_v, g_v, mask_v, bins_v, halo, sent, got, own, bias, weight,
+    load_sem, out_sem, halo_send, halo_recv, term_send, term_recv,
 ):
     scale = 1.0 / math.sqrt(HEAD_DIM)
     rows = q_v.shape[0]
@@ -43,7 +44,12 @@
         return pltpu.make_async_copy(src, dst, load_sem.at[at])
 
     loads = [
-        load(0, queries, q_v), load(1, keys, k_v), load(2, values, v_v), load(3, out_grad, g_v)
+        load(0, keys, k_v),
+        load(1, values, v_v),
+        load(2, queries, q_v),
+        load(3, out_grad, g_v),
+        load(4, mask, mask_v),
+        load(5, bins, bins_v),
     ]
     for copy in loads:
         copy.start()
@@ -51,13 +57,15 @@
     barrier = pltpu.get_barrier_semaphore()
     for side in sides:
         pl.semaphore_signal(barrier, inc=1, device_id=side, device_id_type=MESH)
+    for copy in loads[:2]:
+        copy.wait()
     pl.semaphore_wait(barrier, 2)
 
     def columns(group):
         return pl.ds(pl.multiple_of(group * COLS, COLS), COLS)
 
     def halo_copy(group, kind, side):
-        src = (keys, values)[kind]
+        src = (k_v, v_v)[kind]
         at = (kind * 2 + 1 - side) * GROUPS + group
         return pltpu.make_async_remote_copy(
             src_ref=src.at[:, columns(group)],
@@ -79,6 +87,14 @@
             device_id_type=MESH,
         )
 
+    def out_copy(group, at):
+        src = (attended, query_grad, key_grad, value_grad)[at]
+        dst = (attended_hbm, query_grad_hbm, key_grad_hbm, value_grad_hbm)[at]
+        here = columns(group)
+        return pltpu.make_async_copy(
+            src.at[:, here], dst.at[:, here], out_sem.at[at * GROUPS + group]
+        )
+
     each = [(kind, side) for kind in range(2) for side in range(2)]
 
     def send_halo(group, carry):
@@ -88,11 +104,11 @@
 
     lax.fori_loop(0, GROUPS, send_halo, 0)
 
-    bias[...] = jnp.where(mask[...] == 1, 0.0, MASKED)
-    ratio = NBINS / (bins[...].astype(jnp.float32) + 1.0)
+    for copy in loads[2:]:
+        copy.wait()
+    bias[...] = jnp.where(mask_v[...] == 1, 0.0, MASKED)
+    ratio = NBINS / (bins_v[...].astype(jnp.float32) + 1.0)
     weight[...] = jnp.broadcast_to(ratio, (HEAD_DIM, rows)).T
-    for copy in loads:
-        copy.wait()
 
     def attend(group, carry):
         for kind, side in each:
@@ -127,6 +143,8 @@
                 sent[kind, 1, :, here] = term[2 * rows :].astype(jnp.bfloat16)
         for kind, side in each:
             term_copy(group, kind, side).start()
+        out_copy(group, 0).start()
+        out_copy(group, 1).start()
         return carry
 
     lax.fori_loop(0, GROUPS, attend, 0)
@@ -138,6 +156,7 @@
             here = columns(group)
             total = own[kind, :, here] + got[kind, 0, :, here].astype(jnp.float32)
             grad[:, here] = (total + got[kind, 1, :, here].astype(jnp.float32)).astype(jnp.bfloat16)
+            out_copy(group, 2 + kind).start()
         return carry
 
     lax.fori_loop(0, GROUPS, finish, 0)
@@ -146,38 +165,61 @@
         for kind, side in each:
             halo_copy(group, kind, side).wait_send()
             term_copy(group, kind, side).wait_send()
+        for at in range(4):
+            out_copy(group, at).wait()
         return carry
 
     lax.fori_loop(0, GROUPS, drain, 0)
+
+
+def hand_on(*refs):
+    sources, results, held, in_sem, out_sem = refs[:4], refs[4:8], *refs[8:]
+    rows = sources[0].shape[0] // PIECES
+    ins, outs = [], []
+    for at in range(4):
+        for piece in range(PIECES):
+            here, sem = pl.ds(piece * rows, rows), at * PIECES + piece
+            held_here = held.at[at, here]
+            ins.append(pltpu.make_async_copy(sources[at].at[here], held_here, in_sem.at[sem]))
+            outs.append(pltpu.make_async_copy(held_here, results[at].at[here], out_sem.at[sem]))
+    for copy in ins:
+        copy.start()
+    for arrived, onward in zip(ins, outs):
+        arrived.wait()
+        onward.start()
+    for copy in outs:
+        copy.wait()
 
 
 def local(queries, keys, values, doc_mask, ratio_bins, out_grad):
     rows, width = queries.shape
     result = jax.ShapeDtypeStruct((rows, width), jnp.bfloat16)
-    any_space = pl.BlockSpec(memory_space=pl.ANY)
-    vmem = pl.BlockSpec(memory_space=pltpu.VMEM)
+    hbm = pl.BlockSpec(memory_space=pltpu.HBM)
     block = pltpu.VMEM((rows, width), jnp.bfloat16)
-    return pl.pallas_call(
+    inner = pl.pallas_call(
         kernel,
         out_shape=[result] * 4,
-        in_specs=[any_space] * 4 + [vmem] * 2,
-        out_specs=[vmem] * 4,
+        in_specs=[hbm] * 6,
+        out_specs=[hbm] * 4,
         scratch_shapes=[
-            block, block, block, block,
+            block, block, block, block, block, block, block, block,
+            pltpu.VMEM(doc_mask.shape, doc_mask.dtype),
+            pltpu.VMEM((1, rows), ratio_bins.dtype),
             pltpu.VMEM((2, 2, rows, width), jnp.bfloat16),
             pltpu.VMEM((2, 2, rows, width), jnp.bfloat16),
             pltpu.VMEM((2, 2, rows, width), jnp.bfloat16),
             pltpu.VMEM((2, rows, width), jnp.float32),
             pltpu.VMEM(doc_mask.shape, jnp.float32),
             pltpu.VMEM((rows, HEAD_DIM), jnp.float32),
-            pltpu.SemaphoreType.DMA((4,)),
+            pltpu.SemaphoreType.DMA((6,)),
+            pltpu.SemaphoreType.DMA((4 * GROUPS,)),
             pltpu.SemaphoreType.DMA((4 * GROUPS,)),
             pltpu.SemaphoreType.DMA((4 * GROUPS,)),
             pltpu.SemaphoreType.DMA((4 * GROUPS,)),
             pltpu.SemaphoreType.DMA((4 * GROUPS,)),
         ],
         compiler_params=pltpu.CompilerParams(
-            collective_id=0, has_side_effects=True, vmem_limit_bytes=40 * 2**20
+            collective_id=0, has_side_effects=True, vmem_limit_bytes=60 * 2**20
         ),
         cost_estimate=pl.CostEstimate(
             flops=12 * HEADS * rows * 3 * rows * HEAD_DIM,
@@ -185,6 +227,18 @@
             transcendentals=HEADS * rows * 3 * rows,
         ),
     )(queries, keys, values, out_grad, doc_mask, ratio_bins.reshape(1, rows))
+    return pl.pallas_call(
+        hand_on,
+        out_shape=[result] * 4,
+        in_specs=[hbm] * 4,
+        out_specs=[hbm] * 4,
+        scratch_shapes=[
+            pltpu.VMEM((4, rows, width), jnp.bfloat16),
+            pltpu.SemaphoreType.DMA((4 * PIECES,)),
+            pltpu.SemaphoreType.DMA((4 * PIECES,)),
+        ],
+        compiler_params=pltpu.CompilerParams(vmem_limit_bytes=60 * 2**20),
+    )(*inner)
 
 
 def solution(mesh):

time: 165 us -> 159 us (0.964); the launches traced: 163 us -> 158 us
  local copies, waits for them, and re-layouts: 8.91 us -> 0 us
  Pallas kernels: 153 us -> 158 us
    unnamed x16 -> x0, local copies, waits for them, and re-layouts: 8.91 us -> none
    pallas_call x1 -> x2, Pallas kernels: 153 us -> 158 us  [the longest x1 155 us: local(): pl.pallas_call(kernel, out_shape=[result] * 4, in_specs=[hbm] * 6, out_sp...]
where the time goes in v2:
time: 159 us; the launch traced here: 158 us
  Pallas kernels  158 us (99%)
    pallas_call x1, Pallas kernels, local(): pl.pallas_call(kernel, out_shape=[result] * 4, in_specs=[hbm] * 6, out_sp...  155 us

profile of v2, /device:TPU:56, one launch (start us, length us, event | category | flops | bytes accessed | tf_op | source)
XLA Modules:
  0.0 158.4 jit_solution(4245975898402317419)
XLA Ops:
  0.6 155.2 %shard_map.93 = (bf16[128,2048]{1,0:T(8,128)(2,1)}, bf16[128,2048]{1,0:T(8,128)(2,1)}, bf16[128,2048]{1,0:T(8,128)(2,1)}, bf16[128,2048]{1,0:T(8,128)(2,1)}) custom-call(bf16[128,2048]{1,0:T(8,128)(2,1)} %queries.1, bf16[128,2048]{1,0:T(8,128)(2,1)} %keys.1, bf16[128,2048]{1,0:T(8,128)(2,1)} %values.1, bf16[128,2048]{1,0:T(8,128)(2,1)} %out_grad.1, ...), custom_call_target="tpu_custom_call" | custom-call | flops 1207959552 | bytes 4194304 | tf_op jit(solution)/shard_map/pallas_call | solution.py:199
  155.8 2.6 %shard_map.94 = (bf16[128,2048]{1,0:T(8,128)(2,1)}, bf16[128,2048]{1,0:T(8,128)(2,1)}, bf16[128,2048]{1,0:T(8,128)(2,1)}, bf16[128,2048]{1,0:T(8,128)(2,1)}) custom-call(bf16[128,2048]{1,0:T(8,128)(2,1)} %get-tuple-element.8.refs_0_, bf16[128,2048]{1,0:T(8,128)(2,1)} %get-tuple-element.9.refs_1_, bf16[128,2048]{1,0:T(8,128)(2,1)} %get-tuple-element.10.refs_2_, ...), custom_call_target="tpu_custom_call" | custom-call | tf_op jit(solution)/shard_map/pallas_call | solution.py:230

commit v3 on v2

--- a/solution.py
+++ b/solution.py
@@ -34,7 +34,7 @@
     queries, keys, values, out_grad, mask, bins,
     attended_hbm, query_grad_hbm, key_grad_hbm, value_grad_hbm,
     attended, query_grad, key_grad, value_grad, q_v, k_v, v_v, g_v, mask_v, bins_v, halo, sent, got, own, bias, weight,
-    load_sem, out_sem, halo_send, halo_recv, term_send, term_recv,
+    ready, load_sem, out_sem, halo_send, halo_recv, term_send, term_recv,
 ):
     scale = 1.0 / math.sqrt(HEAD_DIM)
     rows = q_v.shape[0]
@@ -55,11 +55,11 @@
         copy.start()
 
     barrier = pltpu.get_barrier_semaphore()
-    for side in sides:
-        pl.semaphore_signal(barrier, inc=1, device_id=side, device_id_type=MESH)
+    pl.semaphore_signal(barrier, inc=1, device_id=sides[0], device_id_type=MESH)
     for copy in loads[:2]:
         copy.wait()
-    pl.semaphore_wait(barrier, 2)
+    pl.semaphore_wait(barrier, 1)
+    pl.semaphore_signal(ready, inc=1, device_id=sides[1], device_id_type=MESH)
 
     def columns(group):
         return pl.ds(pl.multiple_of(group * COLS, COLS), COLS)
@@ -97,12 +97,14 @@
 
     each = [(kind, side) for kind in range(2) for side in range(2)]
 
-    def send_halo(group, carry):
-        for kind, side in each:
+    def send_halo(side, group, carry):
+        for kind in range(2):
             halo_copy(group, kind, side).start()
         return carry
 
-    lax.fori_loop(0, GROUPS, send_halo, 0)
+    lax.fori_loop(0, GROUPS, functools.partial(send_halo, 1), 0)
+    pl.semaphore_wait(ready, 1)
+    lax.fori_loop(0, GROUPS, functools.partial(send_halo, 0), 0)
 
     for copy in loads[2:]:
         copy.wait()
@@ -211,6 +213,7 @@
             pltpu.VMEM((2, rows, width), jnp.float32),
             pltpu.VMEM(doc_mask.shape, jnp.float32),
             pltpu.VMEM((rows, HEAD_DIM), jnp.float32),
+            pltpu.SemaphoreType.REGULAR,
             pltpu.SemaphoreType.DMA((6,)),
             pltpu.SemaphoreType.DMA((4 * GROUPS,)),
             pltpu.SemaphoreType.DMA((4 * GROUPS,)),

time: 159 us -> 157 us (0.987)
  Pallas kernels: 158 us -> 156 us
    pallas_call x1, Pallas kernels: 155 us -> 153 us  [local(): pl.pallas_call(kernel, out_shape=[result] * 4, in_specs=[hbm] * 6, out_sp...]
where the time goes in v3:
time: 157 us; the launch traced here: 156 us
  Pallas kernels  156 us (99%)
    pallas_call x1, Pallas kernels, local(): pl.pallas_call(kernel, out_shape=[result] * 4, in_specs=[hbm] * 6, out_sp...  153 us

profile of v3, /device:TPU:56, one launch (start us, length us, event | category | flops | bytes accessed | tf_op | source)
XLA Modules:
  0.0 156.3 jit_solution(9307829736045456385)
XLA Ops:
  0.6 153.1 %shard_map.93 = (bf16[128,2048]{1,0:T(8,128)(2,1)}, bf16[128,2048]{1,0:T(8,128)(2,1)}, bf16[128,2048]{1,0:T(8,128)(2,1)}, bf16[128,2048]{1,0:T(8,128)(2,1)}) custom-call(bf16[128,2048]{1,0:T(8,128)(2,1)} %queries.1, bf16[128,2048]{1,0:T(8,128)(2,1)} %keys.1, bf16[128,2048]{1,0:T(8,128)(2,1)} %values.1, bf16[128,2048]{1,0:T(8,128)(2,1)} %out_grad.1, ...), custom_call_target="tpu_custom_call" | custom-call | flops 1207959552 | bytes 4194304 | tf_op jit(solution)/shard_map/pallas_call | solution.py:201
  153.7 2.6 %shard_map.94 = (bf16[128,2048]{1,0:T(8,128)(2,1)}, bf16[128,2048]{1,0:T(8,128)(2,1)}, bf16[128,2048]{1,0:T(8,128)(2,1)}, bf16[128,2048]{1,0:T(8,128)(2,1)}) custom-call(bf16[128,2048]{1,0:T(8,128)(2,1)} %get-tuple-element.8.refs_0_, bf16[128,2048]{1,0:T(8,128)(2,1)} %get-tuple-element.9.refs_1_, bf16[128,2048]{1,0:T(8,128)(2,1)} %get-tuple-element.10.refs_2_, ...), custom_call_target="tpu_custom_call" | custom-call | tf_op jit(solution)/shard_map/pallas_call | solution.py:233

commit v4 on v3

--- a/solution.py
+++ b/solution.py
@@ -11,11 +11,11 @@
 HEADS = 16
 HEAD_DIM = 128
 NBINS = 8
-GROUP = 2
+GROUP = 4
 GROUPS = HEADS // GROUP
 COLS = GROUP * HEAD_DIM
 MASKED = -1e30
-PIECES = 4
+PIECES = 2
 MESH = pl.DeviceIdType.MESH
 
 
@@ -151,6 +151,21 @@
 
     lax.fori_loop(0, GROUPS, attend, 0)
 
+    def drain(group, carry):
+        for kind, side in each:
+            halo_copy(group, kind, side).wait_send()
+        for at in range(2):
+            out_copy(group, at).wait()
+        return carry
+
+    lax.fori_loop(0, GROUPS, drain, 0)
+
+    def settle(group):
+        for kind, side in each:
+            term_copy(group, kind, side).wait_send()
+        for at in range(2, 4):
+            out_copy(group, at).wait()
+
     def finish(group, carry):
         for kind, side in each:
             term_copy(group, kind, side).wait_recv()
@@ -159,19 +174,15 @@
             total = own[kind, :, here] + got[kind, 0, :, here].astype(jnp.float32)
             grad[:, here] = (total + got[kind, 1, :, here].astype(jnp.float32)).astype(jnp.bfloat16)
             out_copy(group, 2 + kind).start()
+
+        @pl.when(group > 0)
+        def _():
+            settle(group - 1)
+
         return carry
 
     lax.fori_loop(0, GROUPS, finish, 0)
-
-    def drain(group, carry):
-        for kind, side in each:
-            halo_copy(group, kind, side).wait_send()
-            term_copy(group, kind, side).wait_send()
-        for at in range(4):
-            out_copy(group, at).wait()
-        return carry
-
-    lax.fori_loop(0, GROUPS, drain, 0)
+    settle(GROUPS - 1)
 
 
 def hand_on(*refs):

time: 157 us -> 156 us (level)
  no operation moved by 1% of the time
where the time goes in v4:
time: 156 us; the launch traced here: 155 us
  Pallas kernels  155 us (99%)
    pallas_call x1, Pallas kernels, local(): pl.pallas_call(kernel, out_shape=[result] * 4, in_specs=[hbm] * 6, out_sp...  152 us

profile of v4, /device:TPU:56, one launch (start us, length us, event | category | flops | bytes accessed | tf_op | source)
XLA Modules:
  0.0 155.5 jit_solution(12810977203428967418)
XLA Ops:
  0.6 152.4 %shard_map.93 = (bf16[128,2048]{1,0:T(8,128)(2,1)}, bf16[128,2048]{1,0:T(8,128)(2,1)}, bf16[128,2048]{1,0:T(8,128)(2,1)}, bf16[128,2048]{1,0:T(8,128)(2,1)}) custom-call(bf16[128,2048]{1,0:T(8,128)(2,1)} %queries.1, bf16[128,2048]{1,0:T(8,128)(2,1)} %keys.1, bf16[128,2048]{1,0:T(8,128)(2,1)} %values.1, bf16[128,2048]{1,0:T(8,128)(2,1)} %out_grad.1, ...), custom_call_target="tpu_custom_call" | custom-call | flops 1207959552 | bytes 4194304 | tf_op jit(solution)/shard_map/pallas_call | solution.py:212
  153.1 2.4 %shard_map.94 = (bf16[128,2048]{1,0:T(8,128)(2,1)}, bf16[128,2048]{1,0:T(8,128)(2,1)}, bf16[128,2048]{1,0:T(8,128)(2,1)}, bf16[128,2048]{1,0:T(8,128)(2,1)}) custom-call(bf16[128,2048]{1,0:T(8,128)(2,1)} %get-tuple-element.8.refs_0_, bf16[128,2048]{1,0:T(8,128)(2,1)} %get-tuple-element.9.refs_1_, bf16[128,2048]{1,0:T(8,128)(2,1)} %get-tuple-element.10.refs_2_, ...), custom_call_target="tpu_custom_call" | custom-call | tf_op jit(solution)/shard_map/pallas_call | solution.py:244

commit v5 on v4

--- a/solution.py
+++ b/solution.py
@@ -11,7 +11,7 @@
 HEADS = 16
 HEAD_DIM = 128
 NBINS = 8
-GROUP = 4
+GROUP = 8
 GROUPS = HEADS // GROUP
 COLS = GROUP * HEAD_DIM
 MASKED = -1e30

time: 156 us -> 155 us (level)
  no operation moved by 1% of the time
where the time goes in v5:
time: 155 us; the launch traced here: 154 us
  Pallas kernels  154 us (99%)
    pallas_call x1, Pallas kernels, local(): pl.pallas_call(kernel, out_shape=[result] * 4, in_specs=[hbm] * 6, out_sp...  151 us

profile of v5, /device:TPU:56, one launch (start us, length us, event | category | flops | bytes accessed | tf_op | source)
XLA Modules:
  0.0 154.5 jit_solution(8867359309304050075)
XLA Ops:
  0.6 151.5 %shard_map.93 = (bf16[128,2048]{1,0:T(8,128)(2,1)}, bf16[128,2048]{1,0:T(8,128)(2,1)}, bf16[128,2048]{1,0:T(8,128)(2,1)}, bf16[128,2048]{1,0:T(8,128)(2,1)}) custom-call(bf16[128,2048]{1,0:T(8,128)(2,1)} %queries.1, bf16[128,2048]{1,0:T(8,128)(2,1)} %keys.1, bf16[128,2048]{1,0:T(8,128)(2,1)} %values.1, bf16[128,2048]{1,0:T(8,128)(2,1)} %out_grad.1, ...), custom_call_target="tpu_custom_call" | custom-call | flops 1207959552 | bytes 4194304 | tf_op jit(solution)/shard_map/pallas_call | solution.py:212
  152.1 2.4 %shard_map.94 = (bf16[128,2048]{1,0:T(8,128)(2,1)}, bf16[128,2048]{1,0:T(8,128)(2,1)}, bf16[128,2048]{1,0:T(8,128)(2,1)}, bf16[128,2048]{1,0:T(8,128)(2,1)}) custom-call(bf16[128,2048]{1,0:T(8,128)(2,1)} %get-tuple-element.8.refs_0_, bf16[128,2048]{1,0:T(8,128)(2,1)} %get-tuple-element.9.refs_1_, bf16[128,2048]{1,0:T(8,128)(2,1)} %get-tuple-element.10.refs_2_, ...), custom_call_target="tpu_custom_call" | custom-call | tf_op jit(solution)/shard_map/pallas_call | solution.py:244
